TPU v7x, 32 devices: a whole 2x2x4 slice. The times are simulated.
32 devices in a mesh: dp: 8 (over z, y), tensor: 4 (over x, core).
Axes of the slice: x: 2, y: 2, z: 4, core: 2. Of those that a mesh axis runs over, the one named last changes fastest.
Arguments:
- acts: bfloat16 [4096, 8192], P('dp'), may hold values from -6 to 6
- grads_out: bfloat16 [4096, 14336], P('dp', 'tensor'), may hold values from -0.09375 to 0.09375
- kept_cols: int32 [128, 96], P(None, 'tensor'), may hold values from 0 to 56, as said below
- row_old: float32 [8192], P('dp'), may hold values from 0.05 to 1.8, as said below
- prior_column_moments: float32 [14336], P('tensor'), may hold values from 0.05 to 0.5
Outputs:
- update: bfloat16 [128, 96, 4096], P('dp', 'tensor')
- row_new: float32 [8192], P('dp')
- col_new: float32 [14336], P('tensor')
Inputs may be any that keep to these rules, and one draw needn't show every extreme that they name: `kept_cols`: live entries of a block row within one index of tensor strictly increase along the slots and precede the empty value 56; each block row keeps 24 // 2 to 24 blocks in each index of tensor, and for each index of tensor some block row keeps exactly 24. `row_old`: Positive.
All inputs are finite; a program needn't handle non-finite values.
Results may differ from a plain program's by a relative error of at most 0.0004.
Values may be sent and summed in bfloat16 or wider, within the bound.
A program may use at most 256 MiB of HBM per device.

v0:
```python
import math

import jax
import jax.numpy as jnp
from jax import lax
from jax.sharding import PartitionSpec as P

D = 8192
FFW = 14336


def sddmm(slab, grads_cols, kept_rows):
    token_count = slab.shape[0]
    group = kept_rows.shape[0]
    nblk = grads_cols.shape[1] // 64
    slot_count = kept_rows.shape[1]
    safe = jnp.minimum(kept_rows, nblk - 1)
    blocks = grads_cols.reshape(token_count, nblk, 64)
    selected_entries = jnp.take(blocks, safe.reshape(-1), axis=1).reshape(
        token_count, group, slot_count, 64
    )
    reshaped_row_blocks = slab.reshape(token_count, group, 64)
    block_outer_product = jnp.einsum(
        "lse,lsuc->suec", reshaped_row_blocks, selected_entries, preferred_element_type=jnp.float32
    )
    live = (kept_rows < nblk)[:, :, None, None]
    block_outer_product = jnp.where(live, block_outer_product, jnp.float32(0.0))
    return block_outer_product.reshape(group, slot_count, 4096)


def block_rows(acts, grads_out, kept_cols, first, count):
    group = math.gcd(count, 8)

    def one_group(index):
        row_start = first + index * group
        slab = lax.dynamic_slice_in_dim(acts, row_start * 64, group * 64, 1)
        kept = lax.dynamic_slice_in_dim(kept_cols, row_start, group, 0)
        return sddmm(slab, grads_out, kept)

    result = lax.map(one_group, jnp.arange(count // group, dtype=jnp.int32))
    return result.reshape(count, kept_cols.shape[1], 4096)


def per_device(acts, grads_out, kept_cols, row_old, prior_column_moments):
    total_rows = kept_cols.shape[0]
    slot_count = kept_cols.shape[1]
    nblk = grads_out.shape[1] // 64
    rows_dev = total_rows // lax.axis_size("dp")
    owned_first = lax.axis_index("dp") * rows_dev
    my_kept = lax.dynamic_slice_in_dim(kept_cols, owned_first, rows_dev, 0)
    partial_all = block_rows(acts, grads_out, kept_cols, 0, total_rows)
    grad = lax.psum_scatter(partial_all, "dp", scatter_dimension=0, tiled=True)
    grad_four = grad.reshape(rows_dev, slot_count, 64, 64)
    squared = grad_four * grad_four
    row_part = jnp.sum(squared, axis=(1, 3)).reshape(rows_dev * 64)
    onehot = (my_kept[:, :, None] == jnp.arange(nblk, dtype=jnp.int32)[None, None, :]).astype(
        jnp.float32
    )
    col_blocks = jnp.sum(squared, axis=2)
    col_part = jnp.einsum(
        "rkg,rkc->cg",
        col_blocks,
        onehot,
        precision=lax.Precision.HIGHEST,
        preferred_element_type=jnp.float32,
    ).reshape(nblk * 64)
    complete_row_moments = lax.psum(row_part, "tensor")
    row_new = 0.6 * row_old + 0.4 * complete_row_moments / FFW
    col_full = lax.psum(col_part, "dp")
    col_new = 0.6 * prior_column_moments + 0.4 * col_full / D
    moment_total = lax.psum(jnp.sum(row_new), "dp")
    mean_row = moment_total / D
    col_view = jnp.einsum(
        "rkc,cg->rkg",
        onehot,
        col_new.reshape(nblk, 64),
        precision=lax.Precision.HIGHEST,
        preferred_element_type=jnp.float32,
    )
    row_view = row_new.reshape(rows_dev, 1, 64, 1)
    rescaled_gradient = grad_four * lax.rsqrt(row_view * col_view[:, :, None, :] / mean_row)
    live = (my_kept < nblk)[:, :, None, None]
    rescaled_gradient = jnp.where(live, rescaled_gradient, jnp.float32(0.0))
    update = rescaled_gradient.astype(jnp.bfloat16).reshape(rows_dev, slot_count, 4096)
    return (update, row_new, col_new)


def solution(mesh):
    in_specs = (P("dp", None), P("dp", "tensor"), P(None, "tensor"), P("dp"), P("tensor"))
    out_specs = (P("dp", "tensor", None), P("dp"), P("tensor"))
    return jax.shard_map(
        per_device, mesh=mesh, in_specs=in_specs, out_specs=out_specs, check_vma=False
    )
```

profile of v0, /device:TPU:0, one launch (start us, length us, event | category | flops | bytes accessed | tf_op | source)
XLA Modules:
  0.0 1461.3 jit_solution(6681810640951955860)
XLA Ops:
  14.0 553.0 %while.12 = (s32[]{:T(128)}, f32[16,8,24,4096]{3,2,1,0:T(8,128)}, s32[16]{0:T(128)S(1)}, s32[128,24]{1,0:T(8,128)S(1)}, bf16[512,3584]{0,1:T(8,128)(2,1)}, /*ind...) while((s32[]{:T(128)}, f32[16,8,24,4096]{3,2,1,0:T(8,128)}, ...), condition=%wide.region_1.2_spmd, body=%wide.region_0.1_spmd.sunk | while | flops 812387392 | bytes 62401520 | solution.py:40
  17.3 10.2 gather_fusion
  27.5 8.2 select_bitcast_fusion.2
  35.7 6.5 copy.35
  51.9 10.2 gather_fusion
  62.1 8.2 select_bitcast_fusion.2
  70.3 6.5 copy.35
  86.5 10.2 gather_fusion
  96.7 8.2 select_bitcast_fusion.2
  121.1 10.2 gather_fusion
  131.3 8.2 select_bitcast_fusion.2
  139.4 6.5 copy.35
  155.6 10.2 gather_fusion
  165.8 8.2 select_bitcast_fusion.2
  174.0 6.5 copy.35
  190.1 10.2 gather_fusion
  200.3 8.2 select_bitcast_fusion.2
  208.5 6.5 copy.35
  224.7 10.2 gather_fusion
  234.9 8.2 select_bitcast_fusion.2
  243.0 6.5 copy.35
  259.2 10.2 gather_fusion
  269.5 8.2 select_bitcast_fusion.2
  277.6 6.5 copy.35
  293.8 10.1 gather_fusion
  303.9 8.2 select_bitcast_fusion.2
  328.4 10.2 gather_fusion
  338.6 8.2 select_bitcast_fusion.2
  363.0 10.2 gather_fusion
  373.2 8.2 select_bitcast_fusion.2
  397.5 10.2 gather_fusion
  407.7 8.2 select_bitcast_fusion.2
  432.1 10.2 gather_fusion
  442.3 8.2 select_bitcast_fusion.2
  466.6 10.2 gather_fusion
  476.9 8.2 select_bitcast_fusion.2
  501.2 10.2 gather_fusion
  511.4 8.2 select_bitcast_fusion.2
  535.8 10.2 gather_fusion
  546.0 8.2 select_bitcast_fusion.2
  567.1 793.2 %reduce-scatter.2.cloned.1.call-done = f32[16,24,4096]{2,1,0:T(8,128)} async-done(((f32[128,24,4096]{2,1,0:T(8,128)}), f32[16,24,4096]{2,1,0:T(8,128)}) %reduce-scatter.2.cloned.1.call-update) | async-done | bytes 6291472 | tf_op jit(solution)/shard_map/reduce_scatter | solution.py:52
  1360.2 6.7 multiply_reduce_fusion
  1366.9 10.8 mul.80
  1377.8 7.4 reduce_sum.37
  1386.2 6.8 psum.21
  1393.6 36.4 %all-reduce = (f32[3584]{0:T(1024)S(1)}, f32[]{:T(128)}) all-reduce(f32[3584]{0:T(1024)S(1)} %reshape.102, f32[]{:T(128)} %get-tuple-element.123), channel_id=1, replica_groups=mesh['dp'=8,'tensor'=4] {'dp'}, use_global_device_ids=true, to_apply=%region_7.8 | all-reduce | flops 3585 | bytes 28680 | tf_op jit(solution)/shard_map/psum | solution.py:69
  1435.7 10.9 mul.82
  1447.7 6.8 select_convert_fusion
  (181 shorter events, 206.6 us)
Async XLA Ops:
  7.2 1353.1 %reduce-scatter.2.cloned.1.call-start = ((), (), s32[]{:S(2)}) async-start(), calls=%async_computation.1 | async-start | bytes 56623104 | tf_op jit(solution)/shard_map/reduce_scatter | solution.py:52
  1377.7 15.2 %copy-start.3 = (f32[1024]{0:T(1024)S(1)}, f32[1024]{0:T(1024)}, u32[]{:S(2)}) copy-start(f32[1024]{0:T(1024)} %param.10) | copy-start | bytes 12292
  1377.7 52.2 %copy-start.1 = (f32[3584]{0:T(1024)S(1)}, f32[3584]{0:T(1024)}, u32[]{:S(2)}) copy-start(f32[3584]{0:T(1024)} %param.11) | copy-start | bytes 43012
  1393.6 53.0 %copy-start.2 = (f32[1024]{0:T(1024)}, f32[1024]{0:T(1024)S(1)}, u32[]{:S(2)}) copy-start(f32[1024]{0:T(1024)S(1)} %get-tuple-element.124) | copy-start | bytes 12292
  1429.9 5.8 copy-start
Sparse Core Ops, SparseCore 0:
  567.2 793.0 reduce-scatter.1
where the time goes:
time: 1460 us
  waiting for transfers between devices  793 us (54%)
  local copies, waits for them, and re-layouts  435 us (30%)
  matrix products  131 us (9%)
  blocking collectives  43.2 us (3%)
  other arithmetic  22.2 us (2%)
  loops' own time  21.4 us (1%)
  between operations  14.8 us (1%)
    reduce_scatter x1, waiting for transfers between devices, per_device(): grad = lax.psum_scatter(partial_all, 'dp', scatter_dimension=0, tiled=True)  793 us
    gather x16, local copies, waits for them, and re-layouts, sddmm(): jnp.take(blocks, safe.reshape(-1), axis=1)  163 us
    dot_general x16, matrix products, sddmm(): jnp.einsum('lse,lsuc->suec', reshaped_row_blocks, selected_entries, prefe...  131 us
    select_n x16, local copies, waits for them, and re-layouts, sddmm(): block_outer_product = jnp.where(live, block_outer_product, jnp.float32(0.0))  105 us
    broadcast_in_dim x16, local copies, waits for them, and re-layouts, block_rows(): result = lax.map(one_group, jnp.arange(count // group, dtype=jnp.int32))  71.2 us
    psum x1, blocking collectives, per_device(): col_full = lax.psum(col_part, 'dp')  36.4 us
    dynamic_update_slice x16, local copies, waits for them, and re-layouts, block_rows(): result = lax.map(one_group, jnp.arange(count // group, dtype=jnp.int32))  30.2 us
  transfers between devices with their start and end apart: 1, of which 1 were waited for; matrix products, arithmetic and copies ran while one was open for 0% of the time, Pallas kernels for 0%

commit v1 on v0

v1 whole, which is shorter than its diff:
```python
import functools

import jax
import jax.numpy as jnp
from jax import lax
from jax.experimental import pallas as pl
from jax.experimental.pallas import tpu as pltpu
from jax.sharding import PartitionSpec as P

D = 8192
FFW = 14336


def select_kernel(nblk, slots, kept_ref, w_ref, rr_ref, cc_ref, out_ref, u_ref, x_ref):
    r = pl.program_id(0)
    row_scale = rr_ref[...]
    for p in range(nblk // 2):
        cols = slice(p * 128, (p + 1) * 128)
        u_ref[p] = w_ref[:, cols] * row_scale * cc_ref[:, cols]
    first = lax.broadcasted_iota(jnp.int32, (32, 128), 1) < 64

    for k in range(slots):
        c = kept_ref[r, k]
        safe = jnp.minimum(c, nblk - 1)
        p = safe // 2
        h = safe % 2
        even = u_ref[p, pl.ds(0, 32, stride=2), :]
        odd = u_ref[p, pl.ds(1, 32, stride=2), :]
        low = jnp.where(first, even, pltpu.roll(odd, 64, 1))
        high = jnp.where(first, pltpu.roll(even, 64, 1), odd)
        block = jnp.where(h == 0, low, high)
        x_ref[k * 32 : (k + 1) * 32, :] = jnp.where(c < nblk, block, 0.0)
    for j in range(32):
        out_ref[0, :, j * 128 : (j + 1) * 128] = x_ref[pl.ds(j, slots, stride=32), :].astype(
            jnp.bfloat16
        )


def select(kept, w, rr, cc):
    rows, slots = kept.shape
    width = w.shape[1]
    nblk = width // 64
    return pl.pallas_call(
        functools.partial(select_kernel, nblk, slots),
        out_shape=jax.ShapeDtypeStruct((rows, slots, 4096), jnp.bfloat16),
        grid_spec=pltpu.PrefetchScalarGridSpec(
            num_scalar_prefetch=1,
            grid=(rows,),
            in_specs=[
                pl.BlockSpec((64, width), lambda r, _: (r, 0)),
                pl.BlockSpec((64, 1), lambda r, _: (r, 0)),
                pl.BlockSpec((1, width), lambda r, _: (0, 0)),
            ],
            out_specs=pl.BlockSpec((1, slots, 4096), lambda r, _: (r, 0, 0)),
            scratch_shapes=[
                pltpu.VMEM((nblk // 2, 64, 128), jnp.float32),
                pltpu.VMEM((slots * 32, 128), jnp.float32),
            ],
        ),
        compiler_params=pltpu.CompilerParams(vmem_limit_bytes=32 * 1024 * 1024),
    )(kept, w, rr, cc)


def finish(w, my_kept, row_old, prior):
    rows_dev = my_kept.shape[0]
    width = w.shape[1]
    nblk = width // 64
    live = (my_kept[:, :, None] == jnp.arange(nblk, dtype=jnp.int32)).any(1)
    mask = jnp.repeat(live, 64, axis=1)[:, None, :]
    w3 = w.reshape(rows_dev, 64, width)
    squared = jnp.where(mask, w3 * w3, 0.0)
    row_part = jnp.sum(squared, axis=2).reshape(rows_dev * 64)
    col_part = jnp.sum(squared, axis=(0, 1))
    share = 0.6 * jnp.sum(row_old) / lax.axis_size("tensor") + 0.4 * jnp.sum(row_part) / FFW
    mean_row = lax.psum(share, ("dp", "tensor")) / D
    row_new = 0.6 * row_old + 0.4 * lax.psum(row_part, "tensor") / FFW
    col_new = 0.6 * prior + 0.4 * lax.psum(col_part, "dp") / D
    rr = lax.rsqrt(row_new).reshape(rows_dev * 64, 1)
    cc = (lax.rsqrt(col_new) * jnp.sqrt(mean_row)).reshape(1, width)
    return select(my_kept, w, rr, cc), row_new, col_new


def per_device(acts, grads_out, kept_cols, row_old, prior):
    n_dp, n_t = lax.axis_size("dp"), lax.axis_size("tensor")
    tokens, width = grads_out.shape
    part = tokens // n_t
    rows_dev = kept_cols.shape[0] // n_dp
    my_kept = lax.dynamic_slice_in_dim(kept_cols, lax.axis_index("dp") * rows_dev, rows_dev, 0)
    mine = lax.dynamic_slice_in_dim(acts, lax.axis_index("tensor") * part, part, 0)
    mine = lax.all_to_all(mine, "dp", split_axis=1, concat_axis=0, tiled=True)
    slab = lax.all_gather(mine, "tensor", axis=0, tiled=False)
    slab = slab.reshape(n_t, n_dp, part, rows_dev * 64).transpose(1, 0, 2, 3)
    slab = slab.reshape(n_t * n_dp * part, rows_dev * 64)
    pieces = []
    half = width // 2
    for first in range(0, width, half):
        g = lax.all_gather(grads_out[:, first : first + half], "dp", axis=0, tiled=True)
        pieces.append(
            lax.dot_general(
                slab, g, (((0,), (0,)), ((), ())), preferred_element_type=jnp.float32
            )
        )
    w = jnp.concatenate(pieces, axis=1)
    return finish(w, my_kept, row_old, prior)


def solution(mesh):
    in_specs = (P("dp", None), P("dp", "tensor"), P(None, "tensor"), P("dp"), P("tensor"))
    out_specs = (P("dp", "tensor", None), P("dp"), P("tensor"))
    return jax.shard_map(
        per_device, mesh=mesh, in_specs=in_specs, out_specs=out_specs, check_vma=False
    )
```

time: 1460 us -> 681 us (0.47)
  local copies, waits for them, and re-layouts: 435 us -> 25.2 us
  waiting for transfers between devices: 793 us -> 429 us
  blocking collectives: 43.2 us -> 137 us
  matrix products: 131 us -> 42.4 us
  loops' own time: 21.4 us -> 0 us
    reduce_scatter x1 -> x0, waiting for transfers between devices: 793 us -> none  [per_device(): grad = lax.psum_scatter(partial_all, 'dp', scatter_dimension=0, tiled=True)]
    all_gather x0 -> x3, waiting for transfers between devices: none -> 428 us  [the longest x2 376 us: per_device(): lax.all_gather(grads_out[:, first:first + half], 'dp', axis=0, tiled=True)]
    gather x16 -> x0, local copies, waits for them, and re-layouts: 163 us -> none  [sddmm(): jnp.take(blocks, safe.reshape(-1), axis=1)]
    select_n x16 -> x0, local copies, waits for them, and re-layouts: 105 us -> none  [sddmm(): block_outer_product = jnp.where(live, block_outer_product, jnp.float32(0.0))]
    dot_general x18 -> x2, matrix products: 131 us -> 42.4 us  [per_device(): lax.dot_general(slab, g, (((0,), (0,)), ((), ())), preferred_element_type...]
    broadcast_in_dim x16 -> x2, local copies, waits for them, and re-layouts: 71.2 us -> 0.41 us  [the longest x1 0.22 us: finish(): squared = jnp.where(mask, w3 * w3, 0.0)]
    all_to_all x0 -> x1, blocking collectives: none -> 55.5 us  [per_device(): mine = lax.all_to_all(mine, 'dp', split_axis=1, concat_axis=0, tiled=True)]
    psum x2 -> x3, blocking collectives: 43.2 us -> 81.5 us  [the longest x1 38.4 us: finish(): mean_row = lax.psum(share, ('dp', 'tensor')) / D]
  transfers between devices with their start and end apart: 1 -> 3, of which waited for: 1 -> 3; matrix products, arithmetic and copies ran while one was open for 0% -> 5% of each run, Pallas kernels for 0% -> 0%
where the time goes in v1:
time: 681 us; the launch traced here: 680 us
  waiting for transfers between devices  429 us (63%)
  blocking collectives  137 us (20%)
  matrix products  42.4 us (6%)
  local copies, waits for them, and re-layouts  25.2 us (4%)
  other arithmetic  19.4 us (3%)
  between operations  15.9 us (2%)
  Pallas kernels  11.6 us (2%)
    all_gather x2, waiting for transfers between devices, per_device(): lax.all_gather(grads_out[:, first:first + half], 'dp', axis=0, tiled=True)  376 us
    all_to_all x1, blocking collectives, per_device(): mine = lax.all_to_all(mine, 'dp', split_axis=1, concat_axis=0, tiled=True)  55.5 us
    all_gather x1, waiting for transfers between devices, per_device(): slab = lax.all_gather(mine, 'tensor', axis=0, tiled=False)  51.8 us
    dot_general x2, matrix products, per_device(): lax.dot_general(slab, g, (((0,), (0,)), ((), ())), preferred_element_type...  42.4 us
    psum x1, blocking collectives, finish(): mean_row = lax.psum(share, ('dp', 'tensor')) / D  38.4 us
    psum x1, blocking collectives, finish(): col_new = 0.6 * prior + 0.4 * lax.psum(col_part, 'dp') / D  37 us
  transfers between devices with their start and end apart: 3, of which 3 were waited for; matrix products, arithmetic and copies ran while one was open for 5% of the time, Pallas kernels for 0%

profile of v1, /device:TPU:0, one launch (start us, length us, event | category | flops | bytes accessed | tf_op | source)
XLA Modules:
  0.0 680.5 jit_solution(16179536659367720206)
XLA Ops:
  7.2 0.0 copy-start
  7.2 0.0 all-gather.4.cloned.1.call-start
  7.2 1.7 constant_dynamic-slice_fusion
  9.0 2.4 copy.32
  11.4 55.5 %all_to_all.16 = bf16[128,8,1024]{0,2,1:T(8,128)(2,1)S(1)} all-to-all(bf16[128,8,1024]{0,2,1:T(8,128)(2,1)} %bitcast.20), channel_id=1, replica_groups=mesh['dp'=8,'tensor'=4] {'dp'}, dimensions={1} | all-to-all | bytes 4194304 | tf_op jit(solution)/shard_map/all_to_all | solution.py:90
  66.9 2.6 copy.28
  69.5 0.0 all-gather.4.cloned.1.call-update
  69.5 0.0 all-gather.6.cloned.1.call-start
  69.6 4.1 fusion.6
  73.7 0.0 all-gather.6.cloned.1.call-update
  73.7 0.0 all-gather.8.cloned.1.call-start
  73.7 0.7 all-gather.8.cloned.1.call-update
  74.4 0.0 copy-done
  74.5 0.1 constant_dynamic-slice_fusion.1
  74.5 0.1 copy.31.kept_ref
  74.6 0.1 fusion.4
  74.7 0.2 broadcast_in_dim.19
  74.9 0.2 broadcast_in_dim.20
  75.2 51.8 %all-gather.4.cloned.1.call-done = bf16[4,1024,1024]{2,1,0:T(8,128)(2,1)} async-done(((bf16[1,1024,1024]{2,1,0:T(8,128)(2,1)}), bf16[4,1024,1024]{2,1,0:T(8,128)(2,1)}) %all-gather.4.cloned.1.call-update) | async-done | bytes 8388624 | tf_op jit(solution)/shard_map/all_gather | solution.py:91
  127.0 8.3 %copy.29 = bf16[8,4,128,1024]{3,2,1,0:T(8,128)(2,1)} copy(bf16[8,4,128,1024]{3,2,0,1:T(8,128)(2,1)} %bitcast.16) | data formatting | bytes 16777216 | tf_op jit(solution)/shard_map/transpose | solution.py:92
  135.3 195.9 %all-gather.6.cloned.1.call-done = bf16[4096,1792]{1,0:T(8,128)(2,1)} async-done(((bf16[512,1792]{1,0:T(8,128)(2,1)}), bf16[4096,1792]{1,0:T(8,128)(2,1)}) %all-gather.6.cloned.1.call-update) | async-done | bytes 14680080 | tf_op jit(solution)/shard_map/all_gather | solution.py:97
  331.2 21.9 %fusion.7 = f32[1024,1792]{1,0:T(8,128)} fusion(bf16[4096,1024]{1,0:T(8,128)(2,1)} %bitcast.17, bf16[4096,1792]{1,0:T(8,128)(2,1)} %all-gather.6.cloned.1.call-done), kind=kOutput, calls=%fused_computation.15 | convolution fusion | flops 15032385536 | bytes 30408704 | tf_op jit(solution)/shard_map/dot_general | solution.py:99
  353.2 180.5 %all-gather.8.cloned.1.call-done = bf16[4096,1792]{1,0:T(8,128)(2,1)} async-done(((bf16[512,1792]{1,0:T(8,128)(2,1)}), bf16[4096,1792]{1,0:T(8,128)(2,1)}) %all-gather.8.cloned.1.call-update) | async-done | bytes 14680080 | tf_op jit(solution)/shard_map/all_gather | solution.py:97
  533.6 0.0 copy-start.3
  533.6 20.4 %fusion.8 = f32[1024,1792]{1,0:T(8,128)S(1)} fusion(bf16[4096,1024]{1,0:T(8,128)(2,1)} %bitcast.18, bf16[4096,1792]{1,0:T(8,128)(2,1)} %all-gather.8.cloned.1.call-done), kind=kOutput, calls=%fused_computation.16 | convolution fusion | flops 15032385536 | bytes 30408704 | tf_op jit(solution)/shard_map/dot_general | solution.py:99
  554.1 0.0 copy-start.4
  554.1 0.0 copy-start.6
  554.1 0.0 copy-done.3
  554.1 6.7 fusion.1
  560.9 0.0 copy-done.4
  560.9 0.1 reduce_sum.39
  560.9 6.1 psum.21
  567.0 0.0 copy-done.6
  567.1 1.2 fusion.5
  569.5 0.0 copy-start.5
  569.6 10.7 %pad_maximum_fusion.w_ref = f32[1024,3584]{1,0:T(8,128)} fusion(f32[1024,1792]{1,0:T(8,128)} %copy-done.4, f32[1024,1792]{1,0:T(8,128)} %fusion.7), kind=kLoop, calls=%fused_computation | loop fusion | flops 3670016 | bytes 29360128 | tf_op jit(solution)/shard_map/concatenate | solution.py:103
  580.2 38.4 %psum.23 = f32[]{:T(128)} all-reduce(f32[]{:T(128)S(6)} %add.25), channel_id=1, replica_groups=mesh['dp'=8,'tensor'=4] {'dp','tensor'}, use_global_device_ids=true, to_apply=%region_7.8 | all-reduce | flops 1 | bytes 8 | tf_op jit(solution)/shard_map/psum | solution.py:75
  619.3 37.0 %psum.22 = f32[3584]{0:T(1024)S(1)} all-reduce(f32[3584]{0:T(1024)S(1)} %get-tuple-element.4), channel_id=1, replica_groups=mesh['dp'=8,'tensor'=4] {'dp'}, use_global_device_ids=true, to_apply=%region_4.5 | all-reduce | flops 3584 | bytes 28672 | tf_op jit(solution)/shard_map/psum | solution.py:77
  656.3 0.0 copy-done.5
  656.3 0.6 rsqrt_multiply_fusion
  656.9 0.0 copy-start.1
  656.9 0.2 copy.30.rr_ref
  657.2 0.0 copy-start.2
  657.2 5.2 copy-done.2
  662.4 11.6 %shard_map.76 = bf16[16,24,4096]{2,1,0:T(8,128)(2,1)} custom-call(s32[16,24]{1,0:T(8,128)S(1)} %copy.31.kept_ref, f32[1024,3584]{1,0:T(8,128)S(1)} %copy-done.2, f32[1024,1]{1,0:T(8,128)S(1)} %copy.30.rr_ref, f32[1,3584]{1,0:T(1,128)S(1)} %reshape.40.cc_ref), custom_call_target="tpu_custom_call" | custom-call | tf_op jit(solution)/shard_map/pallas_call | solution.py:43
  674.0 0.0 copy-done.1
  (1 shorter events, 0.0 us)
Async XLA Ops:
  7.2 67.3 %copy-start = (s32[128,24]{0,1:T(8,128)S(1)}, s32[128,24]{0,1:T(8,128)}, u32[]{:S(2)}) copy-start(s32[128,24]{0,1:T(8,128)} %param.7) | copy-start | bytes 36868
  7.2 119.8 %all-gather.4.cloned.1.call-start = ((), (), s32[]{:S(2)}) async-start(), calls=%async_computation.1 | async-start | bytes 10485760 | tf_op jit(solution)/shard_map/all_gather | solution.py:91
  69.5 261.7 %all-gather.6.cloned.1.call-start = ((), (), s32[]{:S(2)}) async-start(), calls=%async_computation.2 | async-start | bytes 16515072 | tf_op jit(solution)/shard_map/all_gather | solution.py:97
  73.7 459.9 %all-gather.8.cloned.1.call-start = ((), (), s32[]{:S(2)}) async-start(), calls=%async_computation.3 | async-start | bytes 16515072 | tf_op jit(solution)/shard_map/all_gather | solution.py:97
  533.6 20.5 %copy-start.3 = (f32[1024,1792]{1,0:T(8,128)S(1)}, f32[1024,1792]{1,0:T(8,128)}, u32[]{:S(2)}) copy-start(f32[1024,1792]{1,0:T(8,128)} %fusion.7) | copy-start | bytes 22020100
  554.1 6.8 copy-start.4
  554.1 13.0 %copy-start.6 = (f32[1024]{0:T(1024)S(1)}, f32[1024]{0:T(1024)}, u32[]{:S(2)}) copy-start(f32[1024]{0:T(1024)} %param.8) | copy-start | bytes 12292
  569.5 86.8 %copy-start.5 = (f32[3584]{0:T(1024)S(1)}, f32[3584]{0:T(1024)}, u32[]{:S(2)}) copy-start(f32[3584]{0:T(1024)} %param.9) | copy-start | bytes 43012
  656.9 17.0 %copy-start.1 = (s32[128,24]{0,1:T(8,128)S(1)}, s32[128,24]{0,1:T(8,128)}, u32[]{:S(2)}) copy-start(s32[128,24]{0,1:T(8,128)} %param.7) | copy-start | bytes 36868
  657.2 5.2 copy-start.2
Sparse Core Ops, SparseCore 0:
  69.6 57.2 all-gather.3
  129.2 202.0 all-gather.5
  333.4 200.1 all-gather.7

commit v2 on v1

v2 whole, which is shorter than its diff:
```python
import functools

import jax
import jax.numpy as jnp
from jax import lax
from jax.experimental import pallas as pl
from jax.experimental.pallas import tpu as pltpu
from jax.sharding import PartitionSpec as P

D = 8192
FFW = 14336


def select_kernel(nblk, slots, count, kept_ref, *refs):
    w_refs, (rr_ref, cc_ref, out_ref, u_ref, x_ref) = refs[:count], refs[count:]
    r = pl.program_id(0)
    row_scale = rr_ref[...]
    per = nblk // 2 // count
    for p in range(nblk // 2):
        cols = slice(p * 128, (p + 1) * 128)
        here = slice(p % per * 128, (p % per + 1) * 128)
        u_ref[p] = w_refs[p // per][:, here] * row_scale * cc_ref[:, cols]
    first = lax.broadcasted_iota(jnp.int32, (32, 128), 1) < 64

    for k in range(slots):
        c = kept_ref[r, k]
        safe = jnp.minimum(c, nblk - 1)
        p = safe // 2
        h = safe % 2
        even = u_ref[p, pl.ds(0, 32, stride=2), :]
        odd = u_ref[p, pl.ds(1, 32, stride=2), :]
        low = jnp.where(first, even, pltpu.roll(odd, 64, 1))
        high = jnp.where(first, pltpu.roll(even, 64, 1), odd)
        block = jnp.where(h == 0, low, high)
        x_ref[k * 32 : (k + 1) * 32, :] = jnp.where(c < nblk, block, 0.0)
    for j in range(32):
        out_ref[0, :, j * 128 : (j + 1) * 128] = x_ref[pl.ds(j, slots, stride=32), :].astype(
            jnp.bfloat16
        )


def select(kept, w, rr, cc):
    rows, slots = kept.shape
    count = len(w)
    width = cc.shape[1]
    nblk = width // 64
    return pl.pallas_call(
        functools.partial(select_kernel, nblk, slots, count),
        out_shape=jax.ShapeDtypeStruct((rows, slots, 4096), jnp.bfloat16),
        grid_spec=pltpu.PrefetchScalarGridSpec(
            num_scalar_prefetch=1,
            grid=(rows,),
            in_specs=[
                *[pl.BlockSpec((64, width // count), lambda r, _: (r, 0))] * count,
                pl.BlockSpec((64, 1), lambda r, _: (r, 0)),
                pl.BlockSpec((1, width), lambda r, _: (0, 0)),
            ],
            out_specs=pl.BlockSpec((1, slots, 4096), lambda r, _: (r, 0, 0)),
            scratch_shapes=[
                pltpu.VMEM((nblk // 2, 64, 128), jnp.float32),
                pltpu.VMEM((slots * 32, 128), jnp.float32),
            ],
        ),
        compiler_params=pltpu.CompilerParams(vmem_limit_bytes=32 * 1024 * 1024),
    )(kept, *w, rr, cc)


def finish(w, my_kept, row_old, prior):
    rows_dev = my_kept.shape[0]
    width = prior.shape[0]
    nblk = width // 64
    live = (my_kept[:, :, None] == jnp.arange(nblk, dtype=jnp.int32)).any(1)
    mask = jnp.repeat(live, 64, axis=1)[:, None, :]
    row_part, col_parts, first = 0.0, [], 0
    for piece in w:
        last = first + piece.shape[1]
        w3 = piece.reshape(rows_dev, 64, last - first)
        squared = jnp.where(mask[:, :, first:last], w3 * w3, 0.0)
        row_part = row_part + jnp.sum(squared, axis=2).reshape(rows_dev * 64)
        col_parts.append(jnp.sum(squared, axis=(0, 1)))
        first = last
    row_full = jnp.sum(exchange(lambda to: row_part, "tensor"), axis=0)
    row_new = 0.6 * row_old + 0.4 * row_full / FFW
    sums = jnp.concatenate(col_parts + [jnp.broadcast_to(jnp.sum(row_new), (128,))])
    full = jnp.sum(exchange(lambda to: sums, "dp"), axis=0)
    mean_row = full[width] / D
    col_new = 0.6 * prior + 0.4 * full[:width] / D
    rr = lax.rsqrt(row_new).reshape(rows_dev * 64, 1)
    cc = (lax.rsqrt(col_new) * jnp.sqrt(mean_row)).reshape(1, width)
    return select(my_kept, w, rr, cc), row_new, col_new


def exchange(piece_for, axis):
    n = lax.axis_size(axis)
    me = lax.axis_index(axis)
    own = piece_for(me)
    held = jnp.zeros((n,) + own.shape, own.dtype)
    held = lax.dynamic_update_index_in_dim(held, own, me, 0)
    for shift in range(1, n):
        pairs = [(i, (i + shift) % n) for i in range(n)]
        got = lax.ppermute(piece_for((me + shift) % n), axis, pairs)
        held = lax.dynamic_update_index_in_dim(held, got, (me - shift) % n, 0)
    return held


def per_device(acts, grads_out, kept_cols, row_old, prior):
    n_dp, n_t = lax.axis_size("dp"), lax.axis_size("tensor")
    tokens, width = grads_out.shape
    part = tokens // n_t
    rows_dev = kept_cols.shape[0] // n_dp
    own = rows_dev * 64
    my_kept = lax.dynamic_slice_in_dim(kept_cols, lax.axis_index("dp") * rows_dev, rows_dev, 0)
    chunk = width // 2
    gathered = [
        lax.all_gather(grads_out[:, first : first + chunk], "dp", axis=0, tiled=True) for first in range(0, width, chunk)
    ]
    start = lax.axis_index("tensor") * part
    mine = exchange(lambda to: lax.dynamic_slice(acts, (start, to * own), (part, own)), "dp")
    slab = exchange(lambda to: mine, "tensor")
    slab = slab.transpose(1, 0, 2, 3).reshape(n_dp * tokens, own)
    pieces = [
        lax.dot_general(slab, g, (((0,), (0,)), ((), ())), preferred_element_type=jnp.float32)
        for g in gathered
    ]
    return finish(pieces, my_kept, row_old, prior)


def solution(mesh):
    in_specs = (P("dp", None), P("dp", "tensor"), P(None, "tensor"), P("dp"), P("tensor"))
    out_specs = (P("dp", "tensor", None), P("dp"), P("tensor"))
    return jax.shard_map(
        per_device, mesh=mesh, in_specs=in_specs, out_specs=out_specs, check_vma=False
    )
```

time: 681 us -> 529 us (0.78)
  blocking collectives: 137 us -> 0 us
  waiting for transfers between devices: 429 us -> 368 us
  starting transfers between devices: 0.12 us -> 42 us
  other arithmetic: 19.4 us -> 1.42 us
  local copies, waits for them, and re-layouts: 25.2 us -> 40.3 us
    all_gather x3 -> x2, waiting for transfers between devices: 428 us -> 255 us  [per_device(): lax.all_gather(grads_out[:, first:first + chunk], 'dp', axis=0, tiled=True)]
    ppermute x0 -> x20, waiting for transfers between devices: none -> 113 us  [exchange(): got = lax.ppermute(piece_for((me + shift) % n), axis, pairs)]
    psum x3 -> x0, blocking collectives: 81.5 us -> none  [the longest x1 38.4 us: finish(): mean_row = lax.psum(share, ('dp', 'tensor')) / D]
    all_to_all x1 -> x0, blocking collectives: 55.5 us -> none  [per_device(): mine = lax.all_to_all(mine, 'dp', split_axis=1, concat_axis=0, tiled=True)]
    ppermute x0 -> x20, starting transfers between devices: none -> 41.9 us  [exchange(): got = lax.ppermute(piece_for((me + shift) % n), axis, pairs)]
    dynamic_update_slice x0 -> x24, local copies, waits for them, and re-layouts: none -> 20.7 us  [the longest x20 17.6 us: exchange(): held = lax.dynamic_update_index_in_dim(held, got, (me - shift) % n, 0)]
    concatenate x1, other arithmetic: 10.7 us -> 0.01 us  [finish(): jnp.concatenate(col_parts + [jnp.broadcast_to(jnp.sum(row_new), (128,))])]
    transpose x1 -> x0, local copies, waits for them, and re-layouts: 8.3 us -> none  [per_device(): slab = slab.reshape(n_t, n_dp, part, rows_dev * 64).transpose(1, 0, 2, 3)]
  transfers between devices with their start and end apart: 3 -> 22, of which waited for: 3 -> 11; matrix products, arithmetic and copies ran while one was open for 5% -> 10% of each run, Pallas kernels for 0% -> 0%
where the time goes in v2:
time: 529 us; the launch traced here: 528 us
  waiting for transfers between devices  368 us (70%)
  matrix products  49 us (9%)
  starting transfers between devices  42 us (8%)
  local copies, waits for them, and re-layouts  40.3 us (8%)
  between operations  15.4 us (3%)
  Pallas kernels  11.6 us (2%)
    all_gather x2, waiting for transfers between devices, per_device(): lax.all_gather(grads_out[:, first:first + chunk], 'dp', axis=0, tiled=True)  255 us
    ppermute x20, waiting for transfers between devices, exchange(): got = lax.ppermute(piece_for((me + shift) % n), axis, pairs)  113 us
    dot_general x2, matrix products, per_device(): lax.dot_general(slab, g, (((0,), (0,)), ((), ())), preferred_element_type...  49 us
    ppermute x20, starting transfers between devices, exchange(): got = lax.ppermute(piece_for((me + shift) % n), axis, pairs)  41.9 us
    dynamic_update_slice x20, local copies, waits for them, and re-layouts, exchange(): held = lax.dynamic_update_index_in_dim(held, got, (me - shift) % n, 0)  17.6 us
    pallas_call x1, Pallas kernels, select(): pl.pallas_call(functools.partial(select_kernel, nblk, slots, count), out_...  11.6 us
  transfers between devices with their start and end apart: 22, of which 11 were waited for; matrix products, arithmetic and copies ran while one was open for 10% of the time, Pallas kernels for 0%

profile of v2, /device:TPU:0, one launch (start us, length us, event | category | flops | bytes accessed | tf_op | source)
XLA Modules:
  0.0 528.0 jit_solution(14056649984936464519)
XLA Ops:
  7.2 4.2 fusion.9
  11.5 0.7 all-gather.3.cloned.1.call-update
  12.3 2.5 fusion.8
  14.8 3.0 collective-permute-start
  17.8 1.6 collective-permute-start.1
  19.3 2.5 collective-permute-start.2
  21.9 1.2 collective-permute-start.3
  23.1 2.6 collective-permute-start.4
  26.0 1.0 bitcast_dynamic-update-slice_fusion.11
  27.1 1.3 collective-permute-done
  28.4 1.8 collective-permute-start.5
  30.2 1.0 bitcast_dynamic-update-slice_fusion.10
  31.2 12.4 %collective-permute-start.6 = (bf16[128,1024]{1,0:T(8,128)(2,1)S(1)}, bf16[128,1024]{1,0:T(8,128)(2,1)S(1)}, u32[]{:S(2)}, u32[]{:S(2)}) collective-permute-start(bf16[128,1024]{1,0:T(8,128)(2,1)S(1)} %get-tuple-element.11), channel_id=1, source_target_pairs={{0,28},{4,0},{8,4},{12,8},{16,12},{20,16},{24,20},{28,24},{1,29},{... | collective-permute-start | bytes 786440 | tf_op jit(solution)/shard_map/ppermute | solution.py:101
  43.6 1.0 bitcast_dynamic-update-slice_fusion.9
  44.6 20.9 %collective-permute-done.2 = bf16[128,1024]{1,0:T(8,128)(2,1)} collective-permute-done((bf16[128,1024]{1,0:T(8,128)(2,1)S(1)}, bf16[128,1024]{1,0:T(8,128)(2,1)}, u32[]{:S(2)}, u32[]{:S(2)}) %collective-permute-start.2) | collective-permute-done | bytes 262176 | tf_op jit(solution)/shard_map/ppermute | solution.py:101
  65.5 1.0 bitcast_dynamic-update-slice_fusion.8
  66.5 1.0 bitcast_dynamic-update-slice_fusion.7
  67.5 1.0 bitcast_dynamic-update-slice_fusion.6
  68.5 4.3 collective-permute-done.5
  72.8 9.7 %collective-permute-done.6 = bf16[128,1024]{1,0:T(8,128)(2,1)S(1)} collective-permute-done((bf16[128,1024]{1,0:T(8,128)(2,1)S(1)}, bf16[128,1024]{1,0:T(8,128)(2,1)S(1)}, u32[]{:S(2)}, u32[]{:S(2)}) %collective-permute-start.6) | collective-permute-done | bytes 262176 | tf_op jit(solution)/shard_map/ppermute | solution.py:101
  82.7 1.3 collective-permute-start.8
  84.0 1.4 collective-permute-start.9
  86.1 4.4 broadcast_in_dim.120
  90.5 1.7 bitcast_dynamic-update-slice_fusion.2
  92.2 37.8 %collective-permute-done.7 = bf16[8,128,1024]{2,1,0:T(8,128)(2,1)} collective-permute-done((bf16[8,128,1024]{2,1,0:T(8,128)(2,1)S(1)}, bf16[8,128,1024]{2,1,0:T(8,128)(2,1)}, u32[]{:S(2)}, u32[]{:S(2)}) %collective-permute-start.7) | collective-permute-done | bytes 2097184 | tf_op jit(solution)/shard_map/ppermute | solution.py:101
  130.1 3.7 bitcast_dynamic-update-slice_fusion.1
  133.8 3.2 bitcast_dynamic-update-slice_fusion
  137.0 37.3 %collective-permute-done.9 = bf16[8,128,1024]{2,1,0:T(8,128)(2,1)} collective-permute-done((bf16[8,128,1024]{2,1,0:T(8,128)(2,1)S(1)}, bf16[8,128,1024]{2,1,0:T(8,128)(2,1)}, u32[]{:S(2)}, u32[]{:S(2)}) %collective-permute-start.9) | collective-permute-done | bytes 2097184 | tf_op jit(solution)/shard_map/ppermute | solution.py:101
  174.3 3.2 bitcast_dynamic-update-slice_fusion.3
  177.5 76.8 %all-gather.5.cloned.1.call-done = bf16[4096,1792]{1,0:T(8,128)(2,1)} async-done(((bf16[512,1792]{1,0:T(8,128)(2,1)}), bf16[4096,1792]{1,0:T(8,128)(2,1)}) %all-gather.5.cloned.1.call-update) | async-done | bytes 14680080 | tf_op jit(solution)/shard_map/all_gather | solution.py:115
  254.2 24.4 %fusion.2 = (f32[1792]{0:T(1024)S(1)}, f32[1024]{0:T(1024)S(1)}, f32[1024,1792]{1,0:T(8,128)}) fusion(pred[16,1792]{1,0:T(8,128)(4,1)S(1)} %get-tuple-element.20, bf16[4096,1024]{1,0:T(8,128)(2,1)} %bitcast.16, bf16[4096,1792]{1,0:T(8,128)(2,1)} %all-gather.5.cloned.1.call-done), kind=kOutput, calls=%fused_computation.4 | convolution fusion | flops 15039722496 | bytes 30448640 | tf_op jit(solution)/shard_map/dot_general | solution.py:122
  278.6 178.0 %all-gather.3.cloned.1.call-done = bf16[4096,1792]{1,0:T(8,128)(2,1)} async-done(((bf16[512,1792]{1,0:T(8,128)(2,1)}), bf16[4096,1792]{1,0:T(8,128)(2,1)}) %all-gather.3.cloned.1.call-update) | async-done | bytes 14680080 | tf_op jit(solution)/shard_map/all_gather | solution.py:115
  456.7 24.6 %fusion = (f32[1792]{0:T(1024)S(1)}, f32[1024]{0:T(1024)S(1)}, f32[1024,1792]{1,0:T(8,128)}) fusion(pred[16,1792]{1,0:T(8,128)(4,1)S(1)} %get-tuple-element.21, bf16[4096,1024]{1,0:T(8,128)(2,1)} %bitcast.16, bf16[4096,1792]{1,0:T(8,128)(2,1)} %all-gather.3.cloned.1.call-done), kind=kOutput, calls=%fused_computation.2 | convolution fusion | flops 15039722496 | bytes 30448640 | tf_op jit(solution)/shard_map/dot_general | solution.py:122
  481.3 1.5 collective-permute-start.11
  482.8 1.4 collective-permute-start.12
  484.4 0.6 collective-permute-done.11
  485.6 0.6 fusion.7
  486.2 0.6 broadcast_in_dim.147
  486.9 0.6 collective-permute-start.13
  487.5 2.9 collective-permute-start.15
  490.4 1.9 collective-permute-start.16
  492.2 1.0 collective-permute-start.17
  493.4 2.3 collective-permute-start.18
  495.8 2.4 collective-permute-start.19
  502.8 0.6 rsqrt_multiply_fusion
  503.4 3.1 copy-done.2
  506.5 3.1 copy-done.3
  509.6 11.6 %shard_map.76 = bf16[16,24,4096]{2,1,0:T(8,128)(2,1)} custom-call(s32[16,24]{1,0:T(8,128)S(1)} %copy.19.kept_ref, f32[1024,1792]{1,0:T(8,128)S(1)} %copy-done.3, f32[1024,1792]{1,0:T(8,128)S(1)} %copy-done.2, f32[1024,1]{1,0:T(8,128)S(1)} %copy.18.refs_2_, f32[1,3584]{1,0:T(1,128)S(1)} %reshape.47.refs_3_), custom_call_target="tpu_custom_call" | custom-call | tf_op jit(solution)/shard_map/pallas_call | solution.py:47
  (70 shorter events, 5.9 us)
Async XLA Ops:
  7.2 78.2 %copy-start = (s32[128,24]{0,1:T(8,128)S(1)}, s32[128,24]{0,1:T(8,128)}, u32[]{:S(2)}) copy-start(s32[128,24]{0,1:T(8,128)} %param.7) | copy-start | bytes 36868
  7.2 247.0 %all-gather.5.cloned.1.call-start = ((), (), s32[]{:S(2)}) async-start(), calls=%async_computation.1 | async-start | bytes 16515072 | tf_op jit(solution)/shard_map/all_gather | solution.py:115
  11.4 445.2 %all-gather.3.cloned.1.call-start = ((), (), s32[]{:S(2)}) async-start(), calls=%async_computation | async-start | bytes 16515072 | tf_op jit(solution)/shard_map/all_gather | solution.py:115
  14.8 13.6 %collective-permute-start = (bf16[128,1024]{1,0:T(8,128)(2,1)}, bf16[128,1024]{1,0:T(8,128)(2,1)}, u32[]{:S(2)}, u32[]{:S(2)}) collective-permute-start(bf16[128,1024]{1,0:T(8,128)(2,1)} %get-tuple-element.16), channel_id=1, source_target_pairs={{0,4},{4,8},{8,12},{12,16},{16,20},{20,24},{24,28},{28,0},{1,5},{5... | collective-permute-start | bytes 786440 | tf_op jit(solution)/shard_map/ppermute | solution.py:101
  17.8 13.5 %collective-permute-start.1 = (bf16[128,1024]{1,0:T(8,128)(2,1)}, bf16[128,1024]{1,0:T(8,128)(2,1)}, u32[]{:S(2)}, u32[]{:S(2)}) collective-permute-start(bf16[128,1024]{1,0:T(8,128)(2,1)} %get-tuple-element.15), channel_id=1, source_target_pairs={{0,8},{4,12},{8,16},{12,20},{16,24},{20,28},{24,0},{28,4},{1,9},{5... | collective-permute-start | bytes 786440 | tf_op jit(solution)/shard_map/ppermute | solution.py:101
  19.3 46.2 %collective-permute-start.2 = (bf16[128,1024]{1,0:T(8,128)(2,1)S(1)}, bf16[128,1024]{1,0:T(8,128)(2,1)}, u32[]{:S(2)}, u32[]{:S(2)}) collective-permute-start(bf16[128,1024]{1,0:T(8,128)(2,1)S(1)} %get-tuple-element.14), channel_id=1, source_target_pairs={{0,12},{4,16},{8,20},{12,24},{16,28},{20,0},{24,4},{28,8},{1,13},{... | collective-permute-start | bytes 786440 | tf_op jit(solution)/shard_map/ppermute | solution.py:101
  21.9 44.6 %collective-permute-start.3 = (bf16[128,1024]{1,0:T(8,128)(2,1)S(1)}, bf16[128,1024]{1,0:T(8,128)(2,1)}, u32[]{:S(2)}, u32[]{:S(2)}) collective-permute-start(bf16[128,1024]{1,0:T(8,128)(2,1)S(1)} %get-tuple-element.13), channel_id=1, source_target_pairs={{0,16},{4,20},{8,24},{12,28},{16,0},{20,4},{24,8},{28,12},{1,17},{... | collective-permute-start | bytes 786440 | tf_op jit(solution)/shard_map/ppermute | solution.py:101
  23.1 44.4 %collective-permute-start.4 = (bf16[128,1024]{1,0:T(8,128)(2,1)S(1)}, bf16[128,1024]{1,0:T(8,128)(2,1)}, u32[]{:S(2)}, u32[]{:S(2)}) collective-permute-start(bf16[128,1024]{1,0:T(8,128)(2,1)S(1)} %get-tuple-element.12), channel_id=1, source_target_pairs={{0,20},{4,24},{8,28},{12,0},{16,4},{20,8},{24,12},{28,16},{1,21},{... | collective-permute-start | bytes 786440 | tf_op jit(solution)/shard_map/ppermute | solution.py:101
  28.4 44.4 %collective-permute-start.5 = (bf16[128,1024]{1,0:T(8,128)(2,1)S(1)}, bf16[128,1024]{1,0:T(8,128)(2,1)S(1)}, u32[]{:S(2)}, u32[]{:S(2)}) collective-permute-start(bf16[128,1024]{1,0:T(8,128)(2,1)S(1)} %get-tuple-element.17), channel_id=1, source_target_pairs={{0,24},{4,28},{8,0},{12,4},{16,8},{20,12},{24,16},{28,20},{1,25},{... | collective-permute-start | bytes 786440 | tf_op jit(solution)/shard_map/ppermute | solution.py:101
  31.2 51.3 %collective-permute-start.6 = (bf16[128,1024]{1,0:T(8,128)(2,1)S(1)}, bf16[128,1024]{1,0:T(8,128)(2,1)S(1)}, u32[]{:S(2)}, u32[]{:S(2)}) collective-permute-start(bf16[128,1024]{1,0:T(8,128)(2,1)S(1)} %get-tuple-element.11), channel_id=1, source_target_pairs={{0,28},{4,0},{8,4},{12,8},{16,12},{20,16},{24,20},{28,24},{1,29},{... | collective-permute-start | bytes 786440 | tf_op jit(solution)/shard_map/ppermute | solution.py:101
  82.6 47.5 %collective-permute-start.7 = (bf16[8,128,1024]{2,1,0:T(8,128)(2,1)S(1)}, bf16[8,128,1024]{2,1,0:T(8,128)(2,1)}, u32[]{:S(2)}, u32[]{:S(2)}) collective-permute-start(bf16[8,128,1024]{2,1,0:T(8,128)(2,1)S(1)} %bitcast_dynamic-update-slice_fusion.4), channel_id=1, source_target_pairs={{0,1},{1,2},{2,3},{3,0},{4,5},{5,6},{6,7},{7,4},{8,9},{9,10},{10,1... | collective-permute-start | bytes 6291464 | tf_op jit(solution)/shard_map/ppermute | solution.py:101
  82.7 51.1 %collective-permute-start.8 = (bf16[8,128,1024]{2,1,0:T(8,128)(2,1)S(1)}, bf16[8,128,1024]{2,1,0:T(8,128)(2,1)}, u32[]{:S(2)}, u32[]{:S(2)}) collective-permute-start(bf16[8,128,1024]{2,1,0:T(8,128)(2,1)S(1)} %bitcast_dynamic-update-slice_fusion.4), channel_id=1, source_target_pairs={{0,2},{1,3},{2,0},{3,1},{4,6},{5,7},{6,4},{7,5},{8,10},{9,11},{10,... | collective-permute-start | bytes 6291464 | tf_op jit(solution)/shard_map/ppermute | solution.py:101
  84.0 90.3 %collective-permute-start.9 = (bf16[8,128,1024]{2,1,0:T(8,128)(2,1)S(1)}, bf16[8,128,1024]{2,1,0:T(8,128)(2,1)}, u32[]{:S(2)}, u32[]{:S(2)}) collective-permute-start(bf16[8,128,1024]{2,1,0:T(8,128)(2,1)S(1)} %bitcast_dynamic-update-slice_fusion.4), channel_id=1, source_target_pairs={{0,3},{1,0},{2,1},{3,2},{4,7},{5,4},{6,5},{7,6},{8,11},{9,8},{10,9... | collective-permute-start | bytes 6291464 | tf_op jit(solution)/shard_map/ppermute | solution.py:101
  456.7 29.0 %copy-start.6 = (f32[1024]{0:T(1024)S(1)}, f32[1024]{0:T(1024)}, u32[]{:S(2)}) copy-start(f32[1024]{0:T(1024)} %param.8) | copy-start | bytes 12292
  456.7 46.1 %copy-start.5 = (f32[3584]{0:T(1024)S(1)}, f32[3584]{0:T(1024)}, u32[]{:S(2)}) copy-start(f32[3584]{0:T(1024)} %param.9) | copy-start | bytes 43012
  481.3 3.0 collective-permute-start.10
  481.3 3.7 collective-permute-start.11
  482.8 2.7 collective-permute-start.12
  486.2 35.0 %copy-start.4 = (f32[1024]{0:T(1024)}, f32[1024]{0:T(1024)S(1)}, u32[]{:S(2)}) copy-start(f32[1024]{0:T(1024)S(1)} %get-tuple-element.10) | copy-start | bytes 12292
  486.9 6.5 %collective-permute-start.13 = (f32[3712]{0:T(1024)S(1)}, f32[3712]{0:T(1024)S(1)}, u32[]{:S(2)}, u32[]{:S(2)}) collective-permute-start(f32[3712]{0:T(1024)S(1)} %pad_maximum_fusion), channel_id=1, source_target_pairs={{0,4},{4,8},{8,12},{12,16},{16,20},{20,24},{24,28},{28,0},{1,5},{5... | collective-permute-start | bytes 44552 | tf_op jit(solution)/shard_map/ppermute | solution.py:101
  487.5 8.3 %collective-permute-start.14 = (f32[3712]{0:T(1024)S(1)}, f32[3712]{0:T(1024)S(1)}, u32[]{:S(2)}, u32[]{:S(2)}) collective-permute-start(f32[3712]{0:T(1024)S(1)} %pad_maximum_fusion), channel_id=1, source_target_pairs={{0,8},{4,12},{8,16},{12,20},{16,24},{20,28},{24,0},{28,4},{1,9},{5... | collective-permute-start | bytes 44552 | tf_op jit(solution)/shard_map/ppermute | solution.py:101
  487.5 12.0 %collective-permute-start.15 = (f32[3712]{0:T(1024)S(1)}, f32[3712]{0:T(1024)S(1)}, u32[]{:S(2)}, u32[]{:S(2)}) collective-permute-start(f32[3712]{0:T(1024)S(1)} %pad_maximum_fusion), channel_id=1, source_target_pairs={{0,12},{4,16},{8,20},{12,24},{16,28},{20,0},{24,4},{28,8},{1,13},{... | collective-permute-start | bytes 44552 | tf_op jit(solution)/shard_map/ppermute | solution.py:101
  490.4 9.6 %collective-permute-start.16 = (f32[3712]{0:T(1024)S(1)}, f32[3712]{0:T(1024)S(1)}, u32[]{:S(2)}, u32[]{:S(2)}) collective-permute-start(f32[3712]{0:T(1024)S(1)} %pad_maximum_fusion), channel_id=1, source_target_pairs={{0,16},{4,20},{8,24},{12,28},{16,0},{20,4},{24,8},{28,12},{1,17},{... | collective-permute-start | bytes 44552 | tf_op jit(solution)/shard_map/ppermute | solution.py:101
  492.2 8.1 %collective-permute-start.17 = (f32[3712]{0:T(1024)S(1)}, f32[3712]{0:T(1024)S(1)}, u32[]{:S(2)}, u32[]{:S(2)}) collective-permute-start(f32[3712]{0:T(1024)S(1)} %pad_maximum_fusion), channel_id=1, source_target_pairs={{0,20},{4,24},{8,28},{12,0},{16,4},{20,8},{24,12},{28,16},{1,21},{... | collective-permute-start | bytes 44552 | tf_op jit(solution)/shard_map/ppermute | solution.py:101
  493.4 7.3 %collective-permute-start.18 = (f32[3712]{0:T(1024)S(1)}, f32[3712]{0:T(1024)S(1)}, u32[]{:S(2)}, u32[]{:S(2)}) collective-permute-start(f32[3712]{0:T(1024)S(1)} %pad_maximum_fusion), channel_id=1, source_target_pairs={{0,24},{4,28},{8,0},{12,4},{16,8},{20,12},{24,16},{28,20},{1,25},{... | collective-permute-start | bytes 44552 | tf_op jit(solution)/shard_map/ppermute | solution.py:101
  495.8 5.4 %collective-permute-start.19 = (f32[3712]{0:T(1024)S(1)}, f32[3712]{0:T(1024)S(1)}, u32[]{:S(2)}, u32[]{:S(2)}) collective-permute-start(f32[3712]{0:T(1024)S(1)} %pad_maximum_fusion), channel_id=1, source_target_pairs={{0,28},{4,0},{8,4},{12,8},{16,12},{20,16},{24,20},{28,24},{1,29},{... | collective-permute-start | bytes 44552 | tf_op jit(solution)/shard_map/ppermute | solution.py:101
  503.4 3.1 copy-start.2
  506.5 3.1 copy-start.3
  509.6 11.6 %copy-start.1 = (s32[128,24]{0,1:T(8,128)S(1)}, s32[128,24]{0,1:T(8,128)}, u32[]{:S(2)}) copy-start(s32[128,24]{0,1:T(8,128)} %param.7) | copy-start | bytes 36868
Sparse Core Ops, SparseCore 0:
  11.5 242.6 all-gather.4
  256.4 200.1 all-gather.2
